TPU v7x, 512 devices: a whole 4x4x16 slice. The times are simulated.
512 devices in a mesh: clus: 16 (over z_lo, x), dir: 32 (over y, z_hi, core).
Axes of the slice: x: 4, y: 4, z: 16 (z_hi: 4, z_lo: 4; z = z_hi * 4 + z_lo), core: 2. Of those that a mesh axis runs over, the one named last changes fastest.
Arguments:
- child_patterns: float32 [768, 2, 256, 128], P('clus', None, 'dir'), may hold values from -6 to 6
- trans_table: bfloat16 [316, 2, 73728], P(None, None, 'dir'), may hold values from -0.875 to 0.875
- child_parent: int32 [16, 48], P('clus'), may hold values from 0 to 7, never falling along the last dimension, each value on 1 to 8 neighbouring positions
- child_octant: int32 [768], P('clus'), may hold values from 0 to 7
- partner_src: int32 [128, 56], replicated, may hold values from 0 to 127, as said below
- partner_off: int32 [128, 56], replicated, may hold values from 0 to 315
- partner_count: int32 [128], replicated, may hold values from 15 to 56, as said below
Outputs:
- child_incoming: float32 [768, 2, 256, 128], P('clus', None, 'dir')
Inputs may be any that keep to these rules, and one draw needn't show every extreme that they name: `partner_src`: each row lists 56 distinct parent clusters, none equal to the row's own index. `partner_count`: the number of live slots at the head of each row of partner_src and partner_off. On one index of clus, all of its 8 parents have 56 live slots. `child_parent`: Non-decreasing along each row; every one of the 8 parents of the row has 1 to 8 children.
All inputs are finite; a program needn't handle non-finite values.
Results may differ from a plain program's by a relative error of at most 0.0003.
Values sent between devices are 32-bit elements; how exact they have to be, the bound alone decides.
A program may use at most 64 MiB of HBM per device.

v0:
```python
import math
import jax
import jax.numpy as jnp
from jax import lax
from jax.sharding import PartitionSpec as P

NTHETA_C = 128
NPHI_C = 256
NTHETA_P = 192
NPHI_P = 384
phase_scale = 8.0 * math.pi
highest = lax.Precision.HIGHEST


def with_halo(shard, sides, width):
    for axis, dim in sides:
        size, length = (lax.axis_size(axis), shard.shape[dim])
        up = [(i, (i + 1) % size) for i in range(size)]
        down = [(j, i) for i, j in up]
        last = lax.slice_in_dim(shard, length - width, length, axis=dim)
        initial = lax.slice_in_dim(shard, 0, width, axis=dim)
        before = lax.ppermute(last, axis, up)
        after = lax.ppermute(initial, axis, down)
        shard = jnp.concatenate([before, shard, after], axis=dim)
    return shard


def lagrange(offset):
    weights = []
    for anchor in range(5):
        factor = jnp.ones_like(offset)
        for neighbour in range(5):
            if neighbour != anchor:
                factor = factor * (offset - neighbour) / (anchor - neighbour)
        weights.append(factor)
    return weights


def polar_matrix_of(rows_out, rows_in):
    target = (jnp.arange(rows_out, dtype=jnp.float32) + 0.5) * rows_in / rows_out - 0.5
    start_row = jnp.clip(jnp.floor(target + 0.5).astype(jnp.int32) - 2, 0, rows_in - 5)
    weights = lagrange(target - start_row.astype(jnp.float32))
    columns = jnp.arange(rows_in, dtype=jnp.int32)
    matrix = jnp.zeros((rows_out, rows_in), jnp.float32)
    for anchor in range(5):
        matrix = matrix + jnp.where(
            columns[None, :] == (start_row + anchor)[:, None], weights[anchor][:, None], 0.0
        )
    return matrix


def azimuth_matrix_of(out_index, in_index, total_out, total_in):
    target = (out_index * total_in).astype(jnp.float32) / total_out
    nearest = jnp.floor(target + 0.5).astype(jnp.int32)
    weights = lagrange(target - nearest.astype(jnp.float32) + 2.0)
    matrix = jnp.zeros((out_index.shape[0], in_index.shape[0]), jnp.float32)
    for anchor in range(5):
        columns = nearest + anchor - 2
        matrix = matrix + jnp.where(
            in_index[None, :] == columns[:, None], weights[anchor][:, None], 0.0
        )
    return matrix


def shift_phases(octant, azimuth_index, azimuth_total, polar_total):
    azimuth = 2.0 * math.pi * azimuth_index.astype(jnp.float32) / azimuth_total
    polar = math.pi * (jnp.arange(polar_total, dtype=jnp.float32) + 0.5) / polar_total
    first_axis = jnp.sin(polar)[None, :] * jnp.cos(azimuth)[:, None]
    second_axis = jnp.sin(polar)[None, :] * jnp.sin(azimuth)[:, None]
    third_axis = jnp.cos(polar)[None, :] * jnp.ones_like(azimuth)[:, None]
    first_sign = (1 - 2 * (octant % 2)).astype(jnp.float32)
    second_sign = (1 - 2 * (octant // 2 % 2)).astype(jnp.float32)
    third_sign = (1 - 2 * (octant // 4)).astype(jnp.float32)
    phase_angle = phase_scale * (
        first_sign[:, None, None] * first_axis[None]
        + second_sign[:, None, None] * second_axis[None]
        + third_sign[:, None, None] * third_axis[None]
    )
    return (jnp.cos(phase_angle), jnp.sin(phase_angle))


def translate(sources, table, partner_src, partner_off, partner_count):
    live_mask = (
        jnp.arange(partner_src.shape[1], dtype=jnp.int32)[None, :] < partner_count[:, None]
    ).astype(jnp.float32)
    picked = sources[partner_src]
    operator = table[partner_off].astype(jnp.float32) * live_mask[:, :, None, None]
    real_part = jnp.sum(
        operator[:, :, 0] * picked[:, :, 0] - operator[:, :, 1] * picked[:, :, 1], axis=1
    )
    imaginary = jnp.sum(
        operator[:, :, 0] * picked[:, :, 1] + operator[:, :, 1] * picked[:, :, 0], axis=1
    )
    return jnp.stack([real_part, imaginary], axis=1)


def forward_shift(patterns, cosine, sine_part):
    real_part = patterns[:, 0] * cosine - patterns[:, 1] * sine_part
    imaginary = patterns[:, 0] * sine_part + patterns[:, 1] * cosine
    return jnp.stack([real_part, imaginary], axis=1)


def conjugate_shift(patterns, cosine, sine_part):
    real_part = patterns[:, 0] * cosine + patterns[:, 1] * sine_part
    imaginary = patterns[:, 1] * cosine - patterns[:, 0] * sine_part
    return jnp.stack([real_part, imaginary], axis=1)


def on_device(
    child_patterns, trans_table, child_parent, child_octant, partner_src, partner_off, partner_count
):
    child_slots, _, azimuth_in, polar_in = child_patterns.shape
    polar_out = NTHETA_P
    azimuth_out = trans_table.shape[2] // polar_out
    parent_slots = partner_src.shape[0] // lax.axis_size("clus")
    cluster_index = lax.axis_index("clus")
    direction_index = lax.axis_index("dir")
    parents = child_parent[0]
    polar_matrix = polar_matrix_of(NTHETA_P, NTHETA_C)
    onehot = (parents[None, :] == jnp.arange(parent_slots, dtype=jnp.int32)[:, None]).astype(
        jnp.float32
    )
    own_rows = jnp.mod(
        direction_index * azimuth_out + jnp.arange(azimuth_out, dtype=jnp.int32), NPHI_P
    )
    cosine, sine_part = shift_phases(child_octant, own_rows, NPHI_P, polar_out)
    extended = with_halo(child_patterns, (("dir", 2),), 2)
    gather_matrix = azimuth_matrix_of(
        jnp.arange(azimuth_out, dtype=jnp.int32),
        jnp.arange(azimuth_in + 4, dtype=jnp.int32) - 2,
        NPHI_P,
        NPHI_C,
    )
    along_azimuth = jnp.einsum("pc,kacz->kapz", gather_matrix, extended, precision=highest)
    refined = jnp.einsum("kapz,tz->kapt", along_azimuth, polar_matrix, precision=highest)
    shifted = forward_shift(refined, cosine, sine_part)
    radiation = jnp.einsum("gk,kapt->gapt", onehot, shifted, precision=highest)
    flattened = radiation.reshape(parent_slots, 2, azimuth_out * polar_out)
    sources = lax.all_gather(flattened, "clus", axis=0, tiled=True)
    first_row = cluster_index * parent_slots
    own_src = lax.dynamic_slice_in_dim(partner_src, first_row, parent_slots, 0)
    own_off = lax.dynamic_slice_in_dim(partner_off, first_row, parent_slots, 0)
    own_count = lax.dynamic_slice_in_dim(partner_count, first_row, parent_slots, 0)
    incoming = translate(sources, trans_table, own_src, own_off, own_count)
    incoming = incoming.reshape(parent_slots, 2, azimuth_out, polar_out)
    return_matrix = azimuth_matrix_of(
        jnp.arange(azimuth_out + 6, dtype=jnp.int32) - 3,
        jnp.arange(azimuth_in, dtype=jnp.int32),
        NPHI_P,
        NPHI_C,
    )
    per_child = jnp.einsum("gk,gapt->kapt", onehot, incoming, precision=highest)
    returned = conjugate_shift(per_child, cosine, sine_part)
    coarse_own = jnp.einsum("kapt,tz->kapz", returned, polar_matrix, precision=highest)
    coarse = with_halo(coarse_own, (("dir", 2),), 3)
    return jnp.einsum("pc,kapz->kacz", return_matrix, coarse, precision=highest)


def solution(mesh):
    return jax.shard_map(
        on_device,
        mesh=mesh,
        in_specs=(
            P("clus", None, "dir", None),
            P(None, None, "dir"),
            P("clus", None),
            P("clus"),
            P(),
            P(),
            P(),
        ),
        out_specs=P("clus", None, "dir", None),
        check_vma=False,
    )
```

profile of v0, /device:TPU:1, one launch (start us, length us, event | category | flops | bytes accessed | tf_op | source)
XLA Modules:
  0.0 204.3 jit_solution(9964516812942284886)
XLA Ops:
  6.5 0.0 copy-start
  6.5 0.0 all-gather.2.cloned.1.call-start
  6.5 1.3 fusion.124
  7.9 0.0 copy-start.4
  7.9 0.0 copy-start.1
  7.9 0.0 copy-start.2
  7.9 10.3 %collective-permute-start = (f32[48,2,2,128]{3,2,1,0:T(2,128)S(1)}, f32[48,2,2,128]{3,2,1,0:T(2,128)S(1)}, u32[]{:S(2)}, u32[]{:S(2)}) collective-permute-start(f32[48,2,2,128]{3,2,1,0:T(2,128)S(1)} %get-tuple-element.13), channel_id=1, source_target_pairs={{0,1},{1,2},{2,3},{3,4},{4,5},{5,6},{6,7},{7,8},{8,9},{9,10},{10,1... | collective-permute-start | bytes 294920 | tf_op jit(solution)/shard_map/ppermute | solution.py:22
  18.3 1.9 collective-permute-start.1
  20.5 0.1 fusion.113
  20.6 0.7 fusion.106
  21.2 0.1 broadcast_multiply_fusion.1
  21.3 0.0 collective-permute-done
  21.3 6.8 %collective-permute-done.1 = f32[48,2,2,128]{3,2,1,0:T(2,128)S(1)} collective-permute-done((f32[48,2,2,128]{3,2,1,0:T(2,128)S(1)}, f32[48,2,2,128]{3,2,1,0:T(2,128)S(1)}, u32[]{:S(2)}, u32[]{:S(2)}) %collective-permute-start.1) | collective-permute-done | bytes 98336 | tf_op jit(solution)/shard_map/ppermute | solution.py:23
  28.1 2.0 convolution_bitcast_fusion
  30.1 1.5 fusion.14
  31.7 2.6 %multiply_subtract_fusion.1 = (f32[48,1,12,192]{3,0,2,1:T(8,128)S(1)}, f32[48,1,12,192]{3,0,2,1:T(8,128)S(1)}) fusion(f32[48,2,12,192]{3,0,2,1:T(8,128)S(1)} %fusion.14, f32[192]{0:T(256)S(1)} %fusion.102, f32[48]{0:T(128)S(1)} %get-tuple-element.19, f32[12,192]{1,0:T(8,128)S(1)} %get-tuple-element.16, f32[48]{0:T(128)S(1)} %get-tuple-element.18, ...), kind=kLoop, calls=%fused_computation.27 | loop fusion | flops 1327104 | bytes 1789248 | tf_op jit(solution)/shard_map/sub | solution.py:98
  34.3 0.0 copy-done.3
  34.3 0.5 fusion
  34.8 0.1 copy.36
  34.9 0.8 reshape.383
  35.7 0.0 all-gather.2.cloned.1.call-update
  35.8 0.0 copy-done.4
  35.8 0.1 dynamic_slice.10
  35.8 0.1 compare_select_fusion
  35.9 0.1 copy.28
  36.0 0.1 reshape.368
  36.1 0.1 copy.24
  36.1 0.1 reshape.360
  36.2 0.0 copy-done
  36.3 20.4 %gather_fusion = bf16[448,2,2304]{2,1,0:T(2,128)(2,1)} fusion(bf16[316,2,2304]{2,1,0:T(2,128)(2,1)S(1)} %copy-done, s32[1024]{0:T(1024)S(1)} %pad_clamp_fusion.1), kind=kCustom, calls=%fused_computation | custom fusion | bytes 8259328 | tf_op jit(solution)/shard_map/gather | solution.py:87
  56.7 0.1 fusion.86
  56.8 8.4 %convert_multiply_fusion = f32[8,56,2,2304]{3,2,1,0:T(2,128)} fusion(bf16[8,56,2,2304]{3,2,1,0:T(2,128)(2,1)} %bitcast.32, f32[8,56]{1,0:T(8,128)S(1)} %fusion.86), kind=kLoop, calls=%fused_computation.2 | loop fusion | flops 4128768 | bytes 12388096 | tf_op jit(solution)/shard_map/mul | solution.py:87
  65.2 53.1 %all-gather.2.cloned.1.call-done = f32[128,2,2304]{2,1,0:T(2,128)} async-done(((f32[8,2,2304]{2,1,0:T(2,128)}), f32[128,2,2304]{2,1,0:T(2,128)}) %all-gather.2.cloned.1.call-update) | async-done | bytes 2359312 | tf_op jit(solution)/shard_map/all_gather | solution.py:139
  118.2 22.7 %gather_fusion.1 = f32[448,2,2304]{2,1,0:T(2,128)} fusion(f32[128,2,2304]{2,1,0:T(2,128)} %all-gather.2.cloned.1.call-done, s32[1024]{0:T(1024)S(1)} %pad_clamp_fusion), kind=kCustom, calls=%fused_computation.1 | custom fusion | bytes 16516864 | tf_op jit(solution)/shard_map/gather | solution.py:86
  140.9 22.2 %subtract_reduce_fusion = (f32[8,2304]{1,0:T(8,128)S(1)}, f32[8,2304]{1,0:T(8,128)S(1)}) fusion(f32[8,56,2,2304]{3,2,1,0:T(2,128)} %bitcast.31, f32[8,56,2,2304]{3,2,1,0:T(2,128)} %convert_multiply_fusion), kind=kLoop, calls=%fused_computation.4 | loop fusion | flops 8220672 | bytes 16662528 | tf_op jit(solution)/shard_map/reduce_sum | solution.py:88
  163.2 0.1 stack.20
  163.2 0.1 copy.29
  163.3 0.1 stack.21
  163.4 0.1 copy.30
  163.5 0.7 fusion.18
  164.1 2.4 %multiply_add_fusion = (f32[48,1,12,192]{3,0,2,1:T(8,128)S(1)}, f32[48,1,12,192]{3,0,2,1:T(8,128)S(1)}) fusion(f32[48,2,12,192]{3,0,2,1:T(8,128)S(1)} %fusion.18, f32[192]{0:T(256)S(1)} %fusion.102, f32[48]{0:T(128)S(1)} %get-tuple-element.19, f32[12,192]{1,0:T(8,128)S(1)} %get-tuple-element.16, f32[48]{0:T(128)S(1)} %get-tuple-element.18, ...), kind=kLoop, calls=%fused_computation.25 | loop fusion | flops 1327104 | bytes 1789248 | tf_op jit(solution)/shard_map/add | solution.py:104
  166.6 1.4 fusion.4
  168.0 16.7 %collective-permute-start.2 = (f32[48,2,3,128]{3,0,2,1:T(8,128)S(1)}, f32[48,2,3,128]{3,0,2,1:T(8,128)S(1)}, u32[]{:S(2)}, u32[]{:S(2)}) collective-permute-start(f32[48,2,3,128]{3,0,2,1:T(8,128)S(1)} %get-tuple-element.11), channel_id=1, source_target_pairs={{0,1},{1,2},{2,3},{3,4},{4,5},{5,6},{6,7},{7,8},{8,9},{9,10},{10,1... | collective-permute-start | bytes 442376 | tf_op jit(solution)/shard_map/ppermute | solution.py:22
  184.7 1.9 collective-permute-start.3
  186.7 0.1 collective-permute-done.2
  186.8 8.8 %collective-permute-done.3 = f32[48,2,3,128]{3,0,2,1:T(8,128)S(1)} collective-permute-done((f32[48,2,3,128]{3,0,2,1:T(8,128)S(1)}, f32[48,2,3,128]{3,0,2,1:T(8,128)S(1)}, u32[]{:S(2)}, u32[]{:S(2)}) %collective-permute-start.3) | collective-permute-done | bytes 147488 | tf_op jit(solution)/shard_map/ppermute | solution.py:23
  195.6 0.1 pad_maximum_fusion
  195.6 1.8 convolution_bitcast_fusion.1
  (25 shorter events, 0.4 us)
Async XLA Ops:
  6.5 29.7 %copy-start = (bf16[316,2,2304]{2,1,0:T(2,128)(2,1)S(1)}, bf16[316,2,2304]{2,1,0:T(2,128)(2,1)}, u32[]{:S(2)}) copy-start(bf16[316,2,2304]{2,1,0:T(2,128)(2,1)} %param.8) | copy-start | bytes 8736772
  6.5 27.7 %copy-start.3 = (s32[1,48]{1,0:T(1,128)S(1)}, s32[1,48]{1,0:T(1,128)}, u32[]{:S(2)}) copy-start(s32[1,48]{1,0:T(1,128)} %param.9) | copy-start | bytes 580
  6.5 111.7 %all-gather.2.cloned.1.call-start = ((), (), s32[]{:S(2)}) async-start(), calls=%async_computation | async-start | bytes 2506752 | tf_op jit(solution)/shard_map/all_gather | solution.py:139
  7.9 27.9 %copy-start.4 = (s32[128]{0:T(128)S(1)}, s32[128]{0:T(128)}, u32[]{:S(2)}) copy-start(s32[128]{0:T(128)} %param.13) | copy-start | bytes 1540
  7.9 27.9 %copy-start.1 = (s32[128,56]{0,1:T(8,128)S(1)}, s32[128,56]{0,1:T(8,128)}, u32[]{:S(2)}) copy-start(s32[128,56]{0,1:T(8,128)} %param.11) | copy-start | bytes 86020
  7.9 27.9 %copy-start.2 = (s32[128,56]{0,1:T(8,128)S(1)}, s32[128,56]{0,1:T(8,128)}, u32[]{:S(2)}) copy-start(s32[128,56]{0,1:T(8,128)} %param.12) | copy-start | bytes 86020
  7.9 13.4 %collective-permute-start = (f32[48,2,2,128]{3,2,1,0:T(2,128)S(1)}, f32[48,2,2,128]{3,2,1,0:T(2,128)S(1)}, u32[]{:S(2)}, u32[]{:S(2)}) collective-permute-start(f32[48,2,2,128]{3,2,1,0:T(2,128)S(1)} %get-tuple-element.13), channel_id=1, source_target_pairs={{0,1},{1,2},{2,3},{3,4},{4,5},{5,6},{6,7},{7,8},{8,9},{9,10},{10,1... | collective-permute-start | bytes 294920 | tf_op jit(solution)/shard_map/ppermute | solution.py:22
  18.3 9.9 %collective-permute-start.1 = (f32[48,2,2,128]{3,2,1,0:T(2,128)S(1)}, f32[48,2,2,128]{3,2,1,0:T(2,128)S(1)}, u32[]{:S(2)}, u32[]{:S(2)}) collective-permute-start(f32[48,2,2,128]{3,2,1,0:T(2,128)S(1)} %get-tuple-element.14), channel_id=1, source_target_pairs={{1,0},{2,1},{3,2},{4,3},{5,4},{6,5},{7,6},{8,7},{9,8},{10,9},{11,1... | collective-permute-start | bytes 294920 | tf_op jit(solution)/shard_map/ppermute | solution.py:23
  168.0 18.8 %collective-permute-start.2 = (f32[48,2,3,128]{3,0,2,1:T(8,128)S(1)}, f32[48,2,3,128]{3,0,2,1:T(8,128)S(1)}, u32[]{:S(2)}, u32[]{:S(2)}) collective-permute-start(f32[48,2,3,128]{3,0,2,1:T(8,128)S(1)} %get-tuple-element.11), channel_id=1, source_target_pairs={{0,1},{1,2},{2,3},{3,4},{4,5},{5,6},{6,7},{7,8},{8,9},{9,10},{10,1... | collective-permute-start | bytes 442376 | tf_op jit(solution)/shard_map/ppermute | solution.py:22
  184.7 10.8 %collective-permute-start.3 = (f32[48,2,3,128]{3,0,2,1:T(8,128)S(1)}, f32[48,2,3,128]{3,0,2,1:T(8,128)S(1)}, u32[]{:S(2)}, u32[]{:S(2)}) collective-permute-start(f32[48,2,3,128]{3,0,2,1:T(8,128)S(1)} %get-tuple-element.12), channel_id=1, source_target_pairs={{1,0},{2,1},{3,2},{4,3},{5,4},{6,5},{7,6},{8,7},{9,8},{10,9},{11,1... | collective-permute-start | bytes 442376 | tf_op jit(solution)/shard_map/ppermute | solution.py:23
Sparse Core Ops, SparseCore 0:
  35.9 82.3 all-gather.1
where the time goes:
time: 205 us; the launch traced here: 204 us
  waiting for transfers between devices  68.7 us (34%)
  local copies, waits for them, and re-layouts  46 us (22%)
  other arithmetic  37.1 us (18%)
  starting transfers between devices  30.9 us (15%)
  between operations  13.6 us (7%)
  matrix products  7.9 us (4%)
    all_gather x1, waiting for transfers between devices, on_device(): sources = lax.all_gather(flattened, 'clus', axis=0, tiled=True)  53.1 us
    ppermute x2, starting transfers between devices, with_halo(): before = lax.ppermute(last, axis, up)  27 us
    gather x1, local copies, waits for them, and re-layouts, translate(): picked = sources[partner_src]  22.7 us
    reduce_sum x1, other arithmetic, translate(): jnp.sum(operator[:, :, 0] * picked[:, :, 0] - operator[:, :, 1] * picked[...  22.2 us
    gather x1, local copies, waits for them, and re-layouts, translate(): table[partner_off].astype(jnp.float32) * live_mask[:, :, None, None]  20.4 us
    ppermute x2, waiting for transfers between devices, with_halo(): after = lax.ppermute(initial, axis, down)  15.5 us
    mul x1, other arithmetic, translate(): table[partner_off].astype(jnp.float32) * live_mask[:, :, None, None]  8.36 us
  transfers between devices with their start and end apart: 5, of which 4 were waited for; matrix products, arithmetic and copies ran while one was open for 15% of the time, Pallas kernels for 0%

commit v1 on v0

--- a/solution.py
+++ b/solution.py
@@ -136,7 +136,8 @@
     shifted = forward_shift(refined, cosine, sine_part)
     radiation = jnp.einsum("gk,kapt->gapt", onehot, shifted, precision=highest)
     flattened = radiation.reshape(parent_slots, 2, azimuth_out * polar_out)
-    sources = lax.all_gather(flattened, "clus", axis=0, tiled=True)
+    sent = jnp.stack([flattened] * lax.axis_size("clus"))
+    sources = jnp.concatenate(lax.all_to_all(sent, "clus", 0, 0), axis=0)
     first_row = cluster_index * parent_slots
     own_src = lax.dynamic_slice_in_dim(partner_src, first_row, parent_slots, 0)
     own_off = lax.dynamic_slice_in_dim(partner_off, first_row, parent_slots, 0)

time: 205 us -> 159 us (0.78)
  the two profiles are of different devices: /device:TPU:1 before, /device:TPU:37 now
where the time goes in v1:
time: 159 us
  local copies, waits for them, and re-layouts  47.7 us (30%)
  waiting for transfers between devices  42.7 us (27%)
  other arithmetic  36.8 us (23%)
  starting transfers between devices  23.6 us (15%)
  matrix products  7.9 us (5%)
    all_to_all x1, waiting for transfers between devices, on_device(): sources = jnp.concatenate(lax.all_to_all(sent, 'clus', 0, 0), axis=0)  24.5 us
    gather x1, local copies, waits for them, and re-layouts, translate(): picked = sources[partner_src]  22.7 us
    reduce_sum x1, other arithmetic, translate(): jnp.sum(operator[:, :, 0] * picked[:, :, 0] - operator[:, :, 1] * picked[...  22.2 us
    gather x1, local copies, waits for them, and re-layouts, translate(): table[partner_off].astype(jnp.float32) * live_mask[:, :, None, None]  20.4 us
    ppermute x2, waiting for transfers between devices, with_halo(): after = lax.ppermute(initial, axis, down)  15.9 us
    ppermute x2, starting transfers between devices, with_halo(): before = lax.ppermute(last, axis, up)  11.5 us
    mul x1, other arithmetic, translate(): table[partner_off].astype(jnp.float32) * live_mask[:, :, None, None]  8.35 us
    all_to_all x1, starting transfers between devices, on_device(): sources = jnp.concatenate(lax.all_to_all(sent, 'clus', 0, 0), axis=0)  7.71 us
  transfers between devices with their start and end apart: 5, of which 5 were waited for; matrix products, arithmetic and copies ran while one was open for 19% of the time, Pallas kernels for 0%

profile of v1, /device:TPU:37, one launch (start us, length us, event | category | flops | bytes accessed | tf_op | source)
XLA Modules:
  0.0 158.9 jit_solution(4985036024523522615)
XLA Ops:
  0.0 0.0 copy-start
  0.0 1.3 fusion.126
  1.4 9.4 %collective-permute-start = (f32[48,2,2,128]{3,2,1,0:T(2,128)S(1)}, f32[48,2,2,128]{3,2,1,0:T(2,128)S(1)}, u32[]{:S(2)}, u32[]{:S(2)}) collective-permute-start(f32[48,2,2,128]{3,2,1,0:T(2,128)S(1)} %get-tuple-element.13), channel_id=1, source_target_pairs={{0,1},{1,2},{2,3},{3,4},{4,5},{5,6},{6,7},{7,8},{8,9},{9,10},{10,1... | collective-permute-start | bytes 294920 | tf_op jit(solution)/shard_map/ppermute | solution.py:22
  10.7 1.9 %collective-permute-start.1 = (f32[48,2,2,128]{3,2,1,0:T(2,128)S(1)}, f32[48,2,2,128]{3,2,1,0:T(2,128)S(1)}, u32[]{:S(2)}, u32[]{:S(2)}) collective-permute-start(f32[48,2,2,128]{3,2,1,0:T(2,128)S(1)} %get-tuple-element.14), channel_id=1, source_target_pairs={{1,0},{2,1},{3,2},{4,3},{5,4},{6,5},{7,6},{8,7},{9,8},{10,9},{11,1... | collective-permute-start | bytes 294920 | tf_op jit(solution)/shard_map/ppermute | solution.py:23
  13.0 0.1 fusion.115
  13.0 0.7 fusion.108
  13.7 0.1 broadcast_multiply_fusion.1
  13.8 0.2 collective-permute-done
  14.0 6.8 %collective-permute-done.1 = f32[48,2,2,128]{3,2,1,0:T(2,128)S(1)} collective-permute-done((f32[48,2,2,128]{3,2,1,0:T(2,128)S(1)}, f32[48,2,2,128]{3,2,1,0:T(2,128)S(1)}, u32[]{:S(2)}, u32[]{:S(2)}) %collective-permute-start.1) | collective-permute-done | bytes 98336 | tf_op jit(solution)/shard_map/ppermute | solution.py:23
  20.7 2.0 %fusion.9 = f32[48,2,128,12]{2,3,1,0:T(8,128)S(1)} fusion(f32[48,2,2,128]{3,2,1,0:T(2,128)S(1)} %collective-permute-done.1, f32[48,2,8,128]{3,2,1,0:T(8,128)} %param.7, f32[48,2,2,128]{3,2,1,0:T(2,128)S(1)} %collective-permute-done, f32[12]{0:T(128)S(1)} %get-tuple-element.20, f32[12]{0:T(128)S(1)} %get-tuple-element.21, f32[12]{0:T(128)S(1)} %get-tuple-element.22, ...), kind=kOutput, calls=%fused_computation.16 | convolution fusion | flops 21530592 | bytes 1180176 | tf_op jit(solution)/shard_map/pc,kacz->kapz/dot_general | solution.py:134
  22.8 1.5 fusion.15
  24.3 2.4 %multiply_subtract_fusion.1 = (f32[48,1,12,192]{3,0,2,1:T(8,128)S(1)}, f32[48,1,12,192]{3,0,2,1:T(8,128)S(1)}) fusion(f32[48,2,12,192]{3,0,2,1:T(8,128)S(1)} %fusion.15, f32[192]{0:T(256)S(1)} %fusion.104, f32[48]{0:T(128)S(1)} %get-tuple-element.19, f32[12,192]{1,0:T(8,128)S(1)} %get-tuple-element.16, f32[48]{0:T(128)S(1)} %get-tuple-element.18, ...), kind=kLoop, calls=%fused_computation.28 | loop fusion | flops 1327104 | bytes 1789248 | tf_op jit(solution)/shard_map/sub | solution.py:98
  26.7 0.0 copy-done.3
  26.7 0.5 fusion
  27.2 0.0 copy-start.4
  27.3 0.0 copy-start.1
  27.3 0.0 copy-start.2
  27.3 0.1 copy.21
  27.4 0.2 reshape.385
  27.5 2.3 %stack.23 = f32[16,8,2,2304]{3,2,1,0:T(2,128)} broadcast(f32[8,2,2304]{2,1,0:T(2,128)S(1)} %reshape.385), dimensions={1,2,3} | broadcast | bytes 2506752 | tf_op jit(solution)/shard_map/stack | solution.py:139
  29.8 7.7 %all-to-all-start = ((f32[16,8,2,2304]{3,2,1,0:T(2,128)}), f32[16,8,2,2304]{3,2,1,0:T(2,128)}, u32[]{:S(2)}, u32[]{:S(2)}) async-start(f32[16,8,2,2304]{3,2,1,0:T(2,128)} %stack.23), calls=%async_computation | async-start | bytes 4718592 | tf_op jit(solution)/shard_map/all_to_all | solution.py:140
  37.5 0.0 copy-done.4
  37.5 0.1 dynamic_slice.10
  37.6 0.1 compare_select_fusion
  37.7 0.1 copy.12
  37.8 0.1 reshape.370
  37.9 0.1 copy.9
  37.9 0.1 reshape.362
  38.0 0.0 copy-done
  38.0 20.4 %gather_fusion = bf16[448,2,2304]{2,1,0:T(2,128)(2,1)} fusion(bf16[316,2,2304]{2,1,0:T(2,128)(2,1)S(1)} %copy-done, s32[1024]{0:T(1024)S(1)} %pad_clamp_fusion.1), kind=kCustom, calls=%fused_computation | custom fusion | bytes 8259328 | tf_op jit(solution)/shard_map/gather | solution.py:87
  58.5 0.1 fusion.88
  58.6 8.4 %convert_multiply_fusion = f32[8,56,2,2304]{3,2,1,0:T(2,128)} fusion(bf16[8,56,2,2304]{3,2,1,0:T(2,128)(2,1)} %bitcast.34, f32[8,56]{1,0:T(8,128)S(1)} %fusion.88), kind=kLoop, calls=%fused_computation.2 | loop fusion | flops 4128768 | bytes 12388096 | tf_op jit(solution)/shard_map/mul | solution.py:87
  67.0 24.5 %all-to-all-done = f32[16,8,2,2304]{3,2,1,0:T(2,128)} async-done(((f32[16,8,2,2304]{3,2,1,0:T(2,128)}), f32[16,8,2,2304]{3,2,1,0:T(2,128)}, u32[]{:S(2)}, u32[]{:S(2)}) %all-to-all-start) | async-done | bytes 2359328 | tf_op jit(solution)/shard_map/all_to_all | solution.py:140
  91.5 22.7 %gather_fusion.1 = f32[448,2,2304]{2,1,0:T(2,128)} fusion(f32[128,2,2304]{2,1,0:T(2,128)} %bitcast.10, s32[1024]{0:T(1024)S(1)} %pad_clamp_fusion), kind=kCustom, calls=%fused_computation.1 | custom fusion | bytes 16516864 | tf_op jit(solution)/shard_map/gather | solution.py:86
  114.2 22.2 %subtract_reduce_fusion = (f32[8,2304]{1,0:T(8,128)S(1)}, f32[8,2304]{1,0:T(8,128)S(1)}) fusion(f32[8,56,2,2304]{3,2,1,0:T(2,128)} %bitcast.33, f32[8,56,2,2304]{3,2,1,0:T(2,128)} %convert_multiply_fusion), kind=kLoop, calls=%fused_computation.4 | loop fusion | flops 8220672 | bytes 16662528 | tf_op jit(solution)/shard_map/reduce_sum | solution.py:88
  136.3 0.1 stack.24
  136.4 0.1 copy.13
  136.5 0.1 stack.25
  136.6 0.1 copy.14
  136.6 0.7 fusion.20
  137.3 2.4 %multiply_add_fusion = (f32[48,1,12,192]{3,0,2,1:T(8,128)S(1)}, f32[48,1,12,192]{3,0,2,1:T(8,128)S(1)}) fusion(f32[48,2,12,192]{3,0,2,1:T(8,128)S(1)} %fusion.20, f32[192]{0:T(256)S(1)} %fusion.104, f32[48]{0:T(128)S(1)} %get-tuple-element.19, f32[12,192]{1,0:T(8,128)S(1)} %get-tuple-element.16, f32[48]{0:T(128)S(1)} %get-tuple-element.18, ...), kind=kLoop, calls=%fused_computation.26 | loop fusion | flops 1327104 | bytes 1789248 | tf_op jit(solution)/shard_map/add | solution.py:104
  139.8 1.4 fusion.4
  141.2 2.1 %collective-permute-start.2 = (f32[48,2,3,128]{3,0,2,1:T(8,128)S(1)}, f32[48,2,3,128]{3,0,2,1:T(8,128)S(1)}, u32[]{:S(2)}, u32[]{:S(2)}) collective-permute-start(f32[48,2,3,128]{3,0,2,1:T(8,128)S(1)} %get-tuple-element.11), channel_id=1, source_target_pairs={{0,1},{1,2},{2,3},{3,4},{4,5},{5,6},{6,7},{7,8},{8,9},{9,10},{10,1... | collective-permute-start | bytes 442376 | tf_op jit(solution)/shard_map/ppermute | solution.py:22
  143.3 2.4 %collective-permute-start.3 = (f32[48,2,3,128]{3,0,2,1:T(8,128)S(1)}, f32[48,2,3,128]{3,0,2,1:T(8,128)S(1)}, u32[]{:S(2)}, u32[]{:S(2)}) collective-permute-start(f32[48,2,3,128]{3,0,2,1:T(8,128)S(1)} %get-tuple-element.12), channel_id=1, source_target_pairs={{1,0},{2,1},{3,2},{4,3},{5,4},{6,5},{7,6},{8,7},{9,8},{10,9},{11,1... | collective-permute-start | bytes 442376 | tf_op jit(solution)/shard_map/ppermute | solution.py:23
  145.8 2.1 %collective-permute-done.2 = f32[48,2,3,128]{3,0,2,1:T(8,128)S(1)} collective-permute-done((f32[48,2,3,128]{3,0,2,1:T(8,128)S(1)}, f32[48,2,3,128]{3,0,2,1:T(8,128)S(1)}, u32[]{:S(2)}, u32[]{:S(2)}) %collective-permute-start.2) | collective-permute-done | bytes 147488 | tf_op jit(solution)/shard_map/ppermute | solution.py:22
  147.9 9.1 %collective-permute-done.3 = f32[48,2,3,128]{3,0,2,1:T(8,128)S(1)} collective-permute-done((f32[48,2,3,128]{3,0,2,1:T(8,128)S(1)}, f32[48,2,3,128]{3,0,2,1:T(8,128)S(1)}, u32[]{:S(2)}, u32[]{:S(2)}) %collective-permute-start.3) | collective-permute-done | bytes 147488 | tf_op jit(solution)/shard_map/ppermute | solution.py:23
  157.0 0.1 pad_maximum_fusion
  157.1 1.8 %convolution_bitcast_fusion = f32[48,2,8,128]{3,2,1,0:T(8,128)} fusion(f32[48,2,18,128]{3,0,2,1:T(8,128)S(1)} %pad_maximum_fusion, f32[18]{0:T(128)S(1)} %get-tuple-element.42, s32[18]{0:T(128)S(1)} %get-tuple-element.48, f32[18]{0:T(128)S(1)} %get-tuple-element.43, s32[18]{0:T(128)S(1)} %get-tuple-element.49, f32[18]{0:T(128)S(1)} %get-tuple-element.44, ...), kind=kOutput, calls=%fused_computation.5 | convolution fusion | flops 21235680 | bytes 1278672 | tf_op jit(solution)/shard_map/pc,kapz->kacz/dot_general | solution.py:157
  (25 shorter events, 0.4 us)
Async XLA Ops:
  0.0 38.0 %copy-start = (bf16[316,2,2304]{2,1,0:T(2,128)(2,1)S(1)}, bf16[316,2,2304]{2,1,0:T(2,128)(2,1)}, u32[]{:S(2)}) copy-start(bf16[316,2,2304]{2,1,0:T(2,128)(2,1)} %param.8) | copy-start | bytes 8736772
  0.0 26.7 %copy-start.3 = (s32[1,48]{1,0:T(1,128)S(1)}, s32[1,48]{1,0:T(1,128)}, u32[]{:S(2)}) copy-start(s32[1,48]{1,0:T(1,128)} %param.9) | copy-start | bytes 580
  1.4 12.6 %collective-permute-start = (f32[48,2,2,128]{3,2,1,0:T(2,128)S(1)}, f32[48,2,2,128]{3,2,1,0:T(2,128)S(1)}, u32[]{:S(2)}, u32[]{:S(2)}) collective-permute-start(f32[48,2,2,128]{3,2,1,0:T(2,128)S(1)} %get-tuple-element.13), channel_id=1, source_target_pairs={{0,1},{1,2},{2,3},{3,4},{4,5},{5,6},{6,7},{7,8},{8,9},{9,10},{10,1... | collective-permute-start | bytes 294920 | tf_op jit(solution)/shard_map/ppermute | solution.py:22
  10.7 10.0 %collective-permute-start.1 = (f32[48,2,2,128]{3,2,1,0:T(2,128)S(1)}, f32[48,2,2,128]{3,2,1,0:T(2,128)S(1)}, u32[]{:S(2)}, u32[]{:S(2)}) collective-permute-start(f32[48,2,2,128]{3,2,1,0:T(2,128)S(1)} %get-tuple-element.14), channel_id=1, source_target_pairs={{1,0},{2,1},{3,2},{4,3},{5,4},{6,5},{7,6},{8,7},{9,8},{10,9},{11,1... | collective-permute-start | bytes 294920 | tf_op jit(solution)/shard_map/ppermute | solution.py:23
  27.2 10.3 %copy-start.4 = (s32[128]{0:T(128)S(1)}, s32[128]{0:T(128)}, u32[]{:S(2)}) copy-start(s32[128]{0:T(128)} %param.13) | copy-start | bytes 1540
  27.3 10.4 %copy-start.1 = (s32[128,56]{0,1:T(8,128)S(1)}, s32[128,56]{0,1:T(8,128)}, u32[]{:S(2)}) copy-start(s32[128,56]{0,1:T(8,128)} %param.11) | copy-start | bytes 86020
  27.3 10.4 %copy-start.2 = (s32[128,56]{0,1:T(8,128)S(1)}, s32[128,56]{0,1:T(8,128)}, u32[]{:S(2)}) copy-start(s32[128,56]{0,1:T(8,128)} %param.12) | copy-start | bytes 86020
  29.8 61.6 %all-to-all-start = ((f32[16,8,2,2304]{3,2,1,0:T(2,128)}), f32[16,8,2,2304]{3,2,1,0:T(2,128)}, u32[]{:S(2)}, u32[]{:S(2)}) async-start(f32[16,8,2,2304]{3,2,1,0:T(2,128)} %stack.23), calls=%async_computation | async-start | bytes 4718592 | tf_op jit(solution)/shard_map/all_to_all | solution.py:140
  141.2 6.7 %collective-permute-start.2 = (f32[48,2,3,128]{3,0,2,1:T(8,128)S(1)}, f32[48,2,3,128]{3,0,2,1:T(8,128)S(1)}, u32[]{:S(2)}, u32[]{:S(2)}) collective-permute-start(f32[48,2,3,128]{3,0,2,1:T(8,128)S(1)} %get-tuple-element.11), channel_id=1, source_target_pairs={{0,1},{1,2},{2,3},{3,4},{4,5},{5,6},{6,7},{7,8},{8,9},{9,10},{10,1... | collective-permute-start | bytes 442376 | tf_op jit(solution)/shard_map/ppermute | solution.py:22
  143.3 13.7 %collective-permute-start.3 = (f32[48,2,3,128]{3,0,2,1:T(8,128)S(1)}, f32[48,2,3,128]{3,0,2,1:T(8,128)S(1)}, u32[]{:S(2)}, u32[]{:S(2)}) collective-permute-start(f32[48,2,3,128]{3,0,2,1:T(8,128)S(1)} %get-tuple-element.12), channel_id=1, source_target_pairs={{1,0},{2,1},{3,2},{4,3},{5,4},{6,5},{7,6},{8,7},{9,8},{10,9},{11,1... | collective-permute-start | bytes 442376 | tf_op jit(solution)/shard_map/ppermute | solution.py:23
